TPU v7x, 256 devices: a whole 4x4x8 slice. The times are simulated.
256 devices in a mesh: ctx: 32 (over y, z), head: 8 (over x, core).
Axes of the slice: x: 4, y: 4, z: 8, core: 2. Of those that a mesh axis runs over, the one named last changes fastest.
Arguments:
- queries: bfloat16 [32768, 2048], P('ctx', 'head'), may hold values from -6 to 6
- key_vectors: bfloat16 [32768, 2048], P('ctx', 'head'), may hold values from -6 to 6
- value_vectors: bfloat16 [32768, 2048], P('ctx', 'head'), may hold values from -60 to 60
- write_rates: float32 [32768, 16], P('ctx', 'head'), may hold values from 0 to 1
- doc_lengths: int32 [32], replicated, may hold values from 1 to 16384, 32768 in all
- norm_gain: float32 [2048], P('head'), may hold values from 0.5 to 1.5
Outputs:
- normed: bfloat16 [32768, 2048], P('ctx', 'head')
All inputs are finite; a program needn't handle non-finite values.
Results may differ from a plain program's by a relative error of at most 0.0014.
Values sent between devices are 32-bit elements; how exact they have to be, the bound alone decides.
A program may use at most 64 MiB of HBM per device.

v0:
```python
import jax
import jax.numpy as jnp
from jax import lax
from jax.sharding import PartitionSpec as P

BLOCK = 128


highest = lax.Precision.HIGHEST
epsilon = 1e-06


def entering(part, axis, combine, identity):
    place = lax.axis_index(axis)
    gathered = jax.tree.map(lambda a: lax.all_gather(a, axis), part)
    state = jax.tree.map(lambda a, e: jnp.zeros_like(a) + jnp.asarray(e, a.dtype), part, identity)

    def one(lap, state):
        return combine(
            state, jax.tree.map(lambda a: lax.dynamic_index_in_dim(a, lap, 0, False), gathered)
        )

    return lax.fori_loop(0, place, one, state)


def normalize(rows):
    return rows * lax.rsqrt(jnp.sum(rows * rows, axis=-1, keepdims=True) + epsilon)


def document_ids(doc_lengths, positions):
    ends = jnp.cumsum(doc_lengths, dtype=jnp.int32)
    begins = ends - doc_lengths
    return jnp.sum((begins[None, :] <= positions[:, None]).astype(jnp.int32), axis=1) - 1


def combine_pairs(earlier, later):
    mul_early, add_early = earlier
    mul_late, add_late = later
    product = jnp.einsum("hij,hjk->hik", mul_late, mul_early, precision=highest)
    shifted = jnp.einsum("hij,hjk->hik", mul_late, add_early, precision=highest) + add_late
    return (product, shifted)


def local(queries, key_vectors, value_vectors, write_rates, doc_lengths, norm_gain):
    tok_dev = queries.shape[0]
    head_count = write_rates.shape[1]
    head_dim = queries.shape[1] // head_count
    block_count = tok_dev // BLOCK

    def split_heads(matrix):
        return (
            matrix.astype(jnp.float32)
            .reshape(block_count, BLOCK, head_count, head_dim)
            .transpose(0, 2, 1, 3)
        )

    query_blocks = normalize(split_heads(queries))
    key_blocks = normalize(split_heads(key_vectors))
    value_blocks = split_heads(value_vectors)
    rate_blocks = write_rates.reshape(block_count, BLOCK, head_count).transpose(0, 2, 1)
    offset = lax.axis_index("ctx") * tok_dev
    positions = offset + jnp.arange(tok_dev, dtype=jnp.int32)
    doc_here = document_ids(doc_lengths, positions).reshape(block_count, BLOCK)
    block_begin = offset + jnp.arange(block_count, dtype=jnp.int32) * BLOCK - 1
    doc_before = document_ids(doc_lengths, block_begin)
    carry_mask = (doc_here == doc_before[:, None]).astype(jnp.float32)
    last_mask = (doc_here == doc_here[:, -1:]).astype(jnp.float32)
    same_doc = doc_here[:, None, :, None] == doc_here[:, None, None, :]
    rows_index = jnp.arange(BLOCK)
    lower_strict = rows_index[:, None] > rows_index[None, :]
    lower_incl = rows_index[:, None] >= rows_index[None, :]
    key_gram = jnp.einsum("nhcd,nhed->nhce", key_blocks, key_blocks, precision=highest)
    coupling = jnp.where(lower_strict & same_doc, rate_blocks[..., :, None] * key_gram, 0.0)
    system = coupling + jnp.eye(BLOCK, dtype=jnp.float32)
    stacked = jnp.concatenate([key_blocks, value_blocks], axis=-1) * rate_blocks[..., None]
    solved = jax.scipy.linalg.solve_triangular(system, stacked, lower=True, unit_diagonal=True)
    wy_keys = solved[..., :head_dim]
    wy_values = solved[..., head_dim:]
    scores = jnp.einsum("nhcd,nhed->nhce", query_blocks, key_blocks, precision=highest)
    scores = jnp.where(lower_incl & same_doc, scores, 0.0)
    carried_keys = wy_keys * carry_mask[:, None, :, None]
    last_keys = key_blocks * last_mask[:, None, :, None]
    carried_queries = query_blocks * carry_mask[:, None, :, None]
    carry_last = carry_mask[:, -1]
    identity_mat = jnp.broadcast_to(
        jnp.eye(head_dim, dtype=jnp.float32), (head_count, head_dim, head_dim)
    )
    zero_state = jnp.zeros((head_count, head_dim, head_dim), jnp.float32)
    step_mul = carry_last[:, None, None, None] * identity_mat[None] - jnp.einsum(
        "nhcd,nhce->nhde", last_keys, carried_keys, precision=highest
    )
    step_add = jnp.einsum("nhcd,nhce->nhde", last_keys, wy_values, precision=highest)

    def fold_pairs(pair, block_pair):
        return (combine_pairs(pair, block_pair), None)

    (dev_mul, dev_add), _ = lax.scan(fold_pairs, (identity_mat, zero_state), (step_mul, step_add))
    _, entry_state = entering((dev_mul, dev_add), "ctx", combine_pairs, (identity_mat, zero_state))

    def run_one(state, block):
        query_now, score_now, carried_now, value_now, last_now, keep_now = block
        updated = value_now - jnp.einsum("hcd,hde->hce", carried_now, state, precision=highest)
        output = jnp.einsum("hcd,hde->hce", query_now, state, precision=highest)
        output = output + jnp.einsum("hce,hed->hcd", score_now, updated, precision=highest)
        state = keep_now * state + jnp.einsum("hcd,hce->hde", last_now, updated, precision=highest)
        return (state, output)

    _, outputs = lax.scan(
        run_one,
        entry_state,
        (carried_queries, scores, carried_keys, wy_values, last_keys, carry_last),
    )
    outputs = outputs.transpose(0, 2, 1, 3).reshape(tok_dev, head_count * head_dim)
    local_squares = jnp.sum(outputs * outputs, axis=1)
    total_squares = lax.psum(local_squares, "head")
    width_all = head_count * head_dim * lax.axis_size("head")
    scale = lax.rsqrt(total_squares / width_all + epsilon)
    return (outputs * scale[:, None] * norm_gain[None, :]).astype(jnp.bfloat16)


def solution(mesh):
    placed = (
        P("ctx", "head"),
        P("ctx", "head"),
        P("ctx", "head"),
        P("ctx", "head"),
        P(),
        P("head"),
    )
    return jax.shard_map(
        local, mesh=mesh, in_specs=placed, out_specs=P("ctx", "head"), check_vma=False
    )
```

profile of v0, /device:TPU:249, one launch (start us, length us, event | category | flops | bytes accessed | tf_op | source)
XLA Modules:
  0.0 490.3 jit_solution(16350187449445751479)
XLA Ops:
  19.4 4.1 fusion.35
  23.5 158.6 %custom-call.4 = f32[8,2,1,128,128]{3,4,2,1,0:T(8,128)} custom-call(f32[8,2,1,128,128]{4,3,2,1,0:T(8,128)} %fusion.35), custom_call_target="InvertDiagBlocksLowerTriangular" | custom-call | tf_op jit(solution)/shard_map/jit(_solve_triangular)/vmap(vmap())/triangular_solve | solution.py:76
  182.1 2.5 reshape.193
  184.7 2.5 copy.108
  187.2 1.8 maximum_multiply_fusion
  189.1 2.3 fusion.29
  191.4 2.3 fusion.47
  193.7 1.9 fusion.51
  196.6 2.3 convolution_subtract_fusion.1
  199.0 19.9 %while.42 = (s32[]{:T(128)}, f32[2,128,128]{2,1,0:T(8,128)S(1)}, f32[2,128,128]{2,1,0:T(8,128)S(1)}, f32[8,2,128,128]{3,2,1,0:T(8,128)}, f32[8,2,128,128]{3,2,1,0:T(8,128)}) while((s32[]{:T(128)}, f32[2,128,128]{2,1,0:T(8,128)S(1)}, f32[2,128,128]{2,1,0:T(8,128)S(1)}, f32[8,2,128,128]{3,2,1,0:T(8,128)}, ...), condition=%wide.region_5.6_spmd.clone.clone, body=%wide.region_4.5_spmd.clone.sunk.clone | while | flops 100728832 | bytes 1443410 | solution.py:97
  221.4 3.3 convolution_select_fusion
  224.8 70.8 %all-gather.7.cloned.1.call-done = f32[64,128,128]{2,1,0:T(8,128)} async-done(((f32[2,128,128]{2,1,0:T(8,128)}), f32[64,128,128]{2,1,0:T(8,128)}) %all-gather.7.cloned.1.call-update) | async-done | bytes 4194320 | tf_op jit(solution)/shard_map/all_gather | solution.py:15
  295.5 81.7 %all-gather.5.cloned.1.call-done = f32[64,128,128]{2,1,0:T(8,128)} async-done(((f32[2,128,128]{2,1,0:T(8,128)}), f32[64,128,128]{2,1,0:T(8,128)}) %all-gather.5.cloned.1.call-update) | async-done | bytes 4194320 | tf_op jit(solution)/shard_map/all_gather | solution.py:15
  377.2 39.9 %while.40 = (s32[]{:T(128)}, f32[2,128,128]{2,1,0:T(8,128)S(1)}, s32[]{:T(128)}, f32[32,2,128,128]{3,2,1,0:T(8,128)}, f32[32,2,128,128]{3,2,1,0:T(8,128)}) while((s32[]{:T(128)}, f32[2,128,128]{2,1,0:T(8,128)S(1)}, s32[]{:T(128)}, f32[32,2,128,128]{3,2,1,0:T(8,128)}, f32[32,2,128,128]{3,2,1,0:T(8,128)}) %tuple.87), condition=%wide.region_7.8_spmd.clone, body=%wide.region_6.7_spmd.sunk.clone | while | flops 50364420 | bytes 787559 | solution.py:23
  417.1 48.3 %while.41 = (s32[]{:T(128)}, f32[2,128,128]{2,1,0:T(8,128)S(1)}, f32[8,2,128,128]{3,2,1,0:T(8,128)S(1)}, f32[8]{0:T(128)S(1)}, f32[8,2,128,128]{2,3,1,0:T(8,128)...) while((s32[]{:T(128)}, f32[2,128,128]{2,1,0:T(8,128)S(1)}, ...), condition=%wide.region_10.11_spmd.clone, body=%wide.region_9.10_spmd.sunk.clone | while | flops 201457664 | bytes 1968761 | solution.py:108
  420.1 1.8 convolution_add_fusion.11
  426.2 1.8 convolution_add_fusion.11
  432.2 1.8 convolution_add_fusion.11
  438.3 1.8 convolution_add_fusion.11
  444.3 1.8 convolution_add_fusion.11
  450.4 1.8 convolution_add_fusion.11
  456.4 1.8 convolution_add_fusion.11
  462.4 1.8 convolution_add_fusion.11
  465.7 15.9 %psum.7 = f32[1024]{0:T(1024)S(1)} all-reduce(f32[1024]{0:T(1024)S(1)} %bitcast.145), channel_id=1, replica_groups=mesh['ctx'=32,'head'=8] {'head'}, use_global_device_ids=true, to_apply=%region_12.13 | all-reduce | flops 1024 | bytes 8192 | tf_op jit(solution)/shard_map/psum | solution.py:115
  (186 shorter events, 110.1 us)
Async XLA Ops:
  6.5 7.5 %copy-start.4 = (bf16[1024,256]{1,0:T(8,128)(2,1)S(1)}, bf16[1024,256]{1,0:T(8,128)(2,1)}, u32[]{:S(2)}) copy-start(bf16[1024,256]{1,0:T(8,128)(2,1)} %param.13) | copy-start | bytes 1572868
  6.5 289.0 %all-gather.7.cloned.1.call-start = ((), (), s32[]{:S(2)}) async-start(), calls=%async_computation.1 | async-start | bytes 4325376 | tf_op jit(solution)/shard_map/all_gather | solution.py:15
  23.5 163.7 %copy-start.6 = (f32[8,2,128]{2,0,1:T(8,128)S(1)}, f32[8,2,128]{2,0,1:T(8,128)}, u32[]{:S(2)}) copy-start(f32[8,2,128]{2,0,1:T(8,128)} %copy.94) | copy-start | bytes 24580
  187.2 1.9 copy-start.3
  193.7 2.9 copy-start.7
  195.6 1.0 copy-start
  218.8 0.7 copy-start.2
  218.8 0.7 copy-start.1
  218.9 2.6 copy-start.5
  219.5 157.7 %all-gather.5.cloned.1.call-start = ((), (), s32[]{:S(2)}) async-start(), calls=%async_computation | async-start | bytes 4325376 | tf_op jit(solution)/shard_map/all_gather | solution.py:15
  465.5 17.0 %copy-start.8 = (f32[256]{0:T(256)S(1)}, f32[256]{0:T(256)}, u32[]{:S(2)}) copy-start(f32[256]{0:T(256)} %param.17) | copy-start | bytes 3076
Sparse Core Ops, SparseCore 0:
  219.6 75.8 all-gather.6
  298.1 79.0 all-gather.4
where the time goes:
time: 492 us; the launch traced here: 490 us
  other arithmetic  169 us (34%)
  waiting for transfers between devices  153 us (31%)
  matrix products  115 us (23%)
  local copies, waits for them, and re-layouts  21 us (4%)
  blocking collectives  15.9 us (3%)
  between operations  13.6 us (3%)
    another operation x4, other arithmetic, local(): jax.scipy.linalg.solve_triangular(system, stacked, lower=True, unit_diago...  159 us
    all_gather x2, waiting for transfers between devices, entering(): gathered = jax.tree.map(lambda a: lax.all_gather(a, axis), part)  152 us
    dot_general x39, matrix products, combine_pairs(): jnp.einsum('hij,hjk->hik', mul_late, add_early, precision=highest)  48.4 us
    psum x1, blocking collectives, local(): total_squares = lax.psum(local_squares, 'head')  15.9 us
    dot_general x8, matrix products, run_one(): jnp.einsum('hcd,hce->hde', last_now, updated, precision=highest)  14.6 us
    dot_general x8, matrix products, run_one(): jnp.einsum('hcd,hde->hce', carried_now, state, precision=highest)  9.86 us
  transfers between devices with their start and end apart: 2, of which 2 were waited for; matrix products, arithmetic and copies ran while one was open for 1% of the time, Pallas kernels for 0%

commit v1 on v0

v1 whole, which is shorter than its diff:
```python
import functools

import jax
import jax.numpy as jnp
from jax import lax
from jax.experimental import pallas as pl
from jax.experimental.pallas import tpu as pltpu
from jax.sharding import PartitionSpec as P

MESH = pl.DeviceIdType.MESH
F32, BF16 = jnp.float32, jnp.bfloat16
EPS = 1e-6
B = 128
NB = 8
ROWS = 8
WIDTH = 2048


def dotf(a, b):
    return lax.dot_general(a, b, (((1,), (0,)), ((), ())), preferred_element_type=F32)


def dot_nt(a, b):
    return lax.dot_general(a, b, (((1,), (1,)), ((), ())), preferred_element_type=F32)


def dot_tn(a, b):
    return lax.dot_general(a, b, (((0,), (0,)), ((), ())), preferred_element_type=F32)


def split(x):
    hi = x.astype(BF16)
    return hi, (x - hi.astype(F32)).astype(BF16)


def dot3(a, b):
    (ah, al), (bh, bl) = a, b
    return dotf(jnp.concatenate([ah, al], 1), jnp.concatenate([bh, bh], 0)) + dotf(ah, bl)


def combine(later, earlier):
    out = dot3(split(later[:, :B]), split(earlier))
    return jnp.concatenate([out[:, :B], out[:, B:] + later[:, B:]], 1)


def iota(shape, dim):
    return lax.broadcasted_iota(jnp.int32, shape, dim)


def invert(lows):
    row, col = iota((B, B), 0), iota((B, B), 1)
    near = (row // 8) == (col // 8)
    n = len(lows)
    parts = []
    for low in lows:
        c = jnp.sum(jnp.where(near, low, 0.0).reshape(16, 8, B), axis=0)
        hi = c.astype(BF16).astype(F32)
        parts += [hi, c - hi]
    stacked = jnp.concatenate(parts, 0).astype(BF16)
    spread = []
    for m in range(7):
        pick = jnp.where(near & (row % 8 == m), 1.0, 0.0).astype(BF16)
        spread.append(dotf(stacked, pick))
    eye8 = (iota((8, B), 1) % 8 == iota((8, B), 0)).astype(F32)
    inv = []
    for s in range(n):
        t = eye8
        for m in range(7):
            coef = spread[m][16 * s : 16 * s + 8] + spread[m][16 * s + 8 : 16 * s + 16]
            t = t - coef * t[m : m + 1]
        inv.append(jnp.where(near, jnp.concatenate([t] * 16, 0), 0.0))
    lsp = [split(low) for low in lows]
    for size in (8, 16, 32, 64):
        r, c = iota((64, B), 0), iota((64, B), 1)
        keep = (c // size) == 2 * (r // size)
        for s in range(n):
            t4 = inv[s].reshape(64 // size, 2, size, B)
            even, odd = t4[:, 0], t4[:, 1].reshape(64, B)
            x = jnp.where(keep, dot3(split(odd), lsp[s]), 0.0)
            odd = odd - dot3(split(x), split(inv[s]))
            inv[s] = jnp.concatenate(
                [even[:, None], odd.reshape(64 // size, 1, size, B)], 1
            ).reshape(B, B)
    return inv


def kernel(
    doc_ref, q_ref, k_ref, v_ref, rate_ref, gain_ref, o_ref,
    start_ref, wu_ref, map_ref, pre_ref, mat_ref, got_ref, ybuf_ref, ysend_ref, pz_ref,
    sout_ref, sbuf_ref, qp_ref, o1_ref, xsend_ref, xbuf_ref,
    g_send, g_recv, y_send, y_recv, s_send, s_recv, x_send, x_recv,
):
    ctx, head = lax.axis_index("ctx"), lax.axis_index("head")
    y, z = ctx // ROWS, lax.rem(ctx, ROWS)
    core = lax.rem(head, 2)

    def at_z(other):
        return {"ctx": y * ROWS + other}

    def at_y(other):
        return {"ctx": lax.rem(other, 4) * ROWS + z}

    def owner_z(h):
        return 4 * core + 2 * h

    mine = (z // 4 == core) & (lax.rem(z, 2) == 0)
    my_h = lax.rem(z, 4) // 2

    barrier = pltpu.get_barrier_semaphore()
    for i in range(1, ROWS):
        pl.semaphore_signal(barrier, 1, device_id=at_z(lax.rem(z + i, ROWS)), device_id_type=MESH)
    for i in range(1, 4):
        pl.semaphore_signal(barrier, 1, device_id=at_y(y + i), device_id_type=MESH)
    for i in range(1, 8):
        pl.semaphore_signal(barrier, 1, device_id={"head": lax.rem(head + i, 8)}, device_id_type=MESH)

    base = ctx * (NB * B)
    pos = base + iota((NB, B), 0) * B + iota((NB, B), 1)
    begin = jnp.int32(0)
    start = jnp.zeros((NB, B), jnp.int32)
    for m in range(31):
        begin = begin + doc_ref[m]
        start = jnp.where(pos >= begin, begin, start)
    start_f = (start - base).astype(F32)
    start_ref[...] = jnp.concatenate([start_f] * 16, 0).T

    row, col = iota((B, B), 0), iota((B, B), 1)
    row1 = iota((B, 1), 0).astype(F32)
    colf = col.astype(F32)

    def doc_columns(b):
        first = start_ref[:, b : b + 1]
        carry = (first < float(b * B)).astype(F32)
        last = (row1 + float(b * B) >= first[B - 1 : B]).astype(F32)
        return first, carry, last

    def lanes(h):
        return pl.ds(pl.multiple_of(h * B, B), B)

    def rate(b, h):
        r = rate_ref[pl.ds(b * B, B), :]
        return jnp.where(h == 0, r[:, 0:1], r[:, 1:2])

    def own_map(h):
        lows, rights = [], []
        for b in range(NB):
            kb = k_ref[pl.ds(b * B, B), lanes(h)]
            kf = kb.astype(F32)
            vf = v_ref[pl.ds(b * B, B), lanes(h)].astype(F32)
            rk = lax.rsqrt(jnp.sum(kf * kf, axis=1, keepdims=True) + EPS)
            beta = rate(b, h)
            first, _, _ = doc_columns(b)
            keep = (row > col) & (colf + float(b * B) >= first)
            scale = beta * rk
            lows.append(jnp.where(keep, dot_nt(kb, kb) * (scale * rk), 0.0))
            rights.append(split(jnp.concatenate([kf * (scale * rk), vf * scale], 1)))
        inv = invert(lows)
        maps = []
        for b in range(NB):
            wu = dot3(split(inv[b]), rights[b])
            _, carry, last = doc_columns(b)
            w, u = wu[:, :B] * carry, wu[:, B:]
            wu_ref[h, b] = jnp.concatenate([w, u], 1)
            hi, lo = split(jnp.concatenate([w * last, u * last], 1))
            kb = k_ref[pl.ds(b * B, B), lanes(h)]
            ma = dot_tn(jnp.concatenate([kb, kb], 0), jnp.concatenate([hi, lo], 0))
            m = jnp.where(row == col, carry[B - 1 : B], 0.0) - ma[:, :B]
            maps.append(jnp.concatenate([m, ma[:, B:]], 1))
            map_ref[h, b] = maps[b]
        pairs = [combine(maps[i + 1], maps[i]) for i in range(0, NB, 2)]
        p03 = combine(pairs[1], pairs[0])
        p47 = combine(pairs[3], pairs[2])
        total = combine(p47, p03)
        mat_ref[h, 0] = total[:, :B]
        mat_ref[h, 1] = total[:, B:]
        pre_ref[h, 1] = pairs[0]
        pre_ref[h, 3] = p03
        pre_ref[h, 4] = pairs[2]


    def send_map(h, part):
        return pltpu.make_async_remote_copy(
            src_ref=mat_ref.at[h, part], dst_ref=got_ref.at[z, part],
            send_sem=g_send.at[h, part], recv_sem=g_recv.at[z, part],
            device_id=at_z(owner_z(h)), device_id_type=MESH,
        )

    for h in range(2):
        own_map(h)
        if h == 0:
            pl.semaphore_wait(barrier, 17)

        @pl.when(z != owner_z(h))
        def _():
            send_map(h, 0).start()
            send_map(h, 1).start()

        @pl.when(z == owner_z(h))
        def _():
            got_ref[z] = mat_ref[h]

    def shadow(h):
        pre = [None, map_ref[h, 0], pre_ref[h, 1], None, pre_ref[h, 3], None, None, None]
        pre[3] = combine(map_ref[h, 2], pre[2])
        pre[5] = combine(map_ref[h, 4], pre[4])
        pre[6] = combine(pre_ref[h, 4], pre[4])
        pre[7] = combine(map_ref[h, 6], pre[6])
        for b in range(NB):
            kb = k_ref[pl.ds(b * B, B), lanes(h)]
            qb = q_ref[pl.ds(b * B, B), lanes(h)]
            qf = qb.astype(F32)
            rq = lax.rsqrt(jnp.sum(qf * qf, axis=1, keepdims=True) + EPS)
            first, carry, _ = doc_columns(b)
            keep = (row >= col) & (colf + float(b * B) >= first)
            sc = jnp.where(keep, dot_nt(qb, kb) * rq, 0.0)
            swu = dot3(split(sc), split(wu_ref[h, b]))
            qe = qf * (rq * carry) - swu[:, :B]
            o1 = swu[:, B:]
            if b > 0:
                qx = dot3(split(qe), split(pre[b]))
                qe = qx[:, :B]
                o1 = o1 + qx[:, B:]
            hi, lo = split(qe)
            qp_ref[h, pl.ds(b * B, B)] = jnp.concatenate([hi, lo], 1)
            o1_ref[h, pl.ds(b * B, B)] = o1

    for h in range(2):
        shadow(h)

    def send_y(src, slot, step):
        return pltpu.make_async_remote_copy(
            src_ref=ysend_ref.at[src], dst_ref=ybuf_ref.at[slot],
            send_sem=y_send.at[slot], recv_sem=y_recv.at[slot],
            device_id=at_y(y + step), device_id_type=MESH,
        )

    def send_state(i):
        to = lax.rem(z + i, ROWS)
        return pltpu.make_async_remote_copy(
            src_ref=sout_ref.at[to], dst_ref=sbuf_ref.at[my_h],
            send_sem=s_send.at[to], recv_sem=s_recv.at[my_h],
            device_id=at_z(to), device_id_type=MESH,
        )

    @pl.when(mine)
    def _():
        for i in range(1, ROWS):
            frm = lax.rem(z + i, ROWS)
            for part in range(2):
                pltpu.make_async_remote_copy(
                    src_ref=mat_ref.at[0, part], dst_ref=got_ref.at[frm, part],
                    send_sem=g_send.at[0, part], recv_sem=g_recv.at[frm, part],
                    device_id=at_z(frm), device_id_type=MESH,
                ).wait_recv()
        maps = [jnp.concatenate([got_ref[i, 0], got_ref[i, 1]], 1) for i in range(ROWS)]
        pairs = [combine(maps[i + 1], maps[i]) for i in range(0, ROWS, 2)]
        p03 = combine(pairs[1], pairs[0])
        p47 = combine(pairs[3], pairs[2])
        total = combine(p47, p03)
        ysend_ref[0] = total[:, :B]
        ysend_ref[1] = total[:, B:]
        sends = [send_y(0, 0, 1), send_y(1, 1, 1), send_y(1, 2, 2)]
        for c in sends:
            c.start()
        pre = [None, maps[0], pairs[0], None, p03, None, None, None]
        pre[3] = combine(maps[2], pre[2])
        pre[5] = combine(maps[4], pre[4])
        pre[6] = combine(pairs[2], pre[4])
        pre[7] = combine(maps[6], pre[6])
        for i in range(1, ROWS):
            pz_ref[i] = pre[i]
        for c in sends:
            c.wait()
        s_row = ybuf_ref[1] + dot3(split(ybuf_ref[0]), split(ybuf_ref[2]))
        sout_ref[0] = s_row
        s_split = split(s_row)
        for i in range(1, ROWS):
            p = pz_ref[i]
            sout_ref[i] = p[:, B:] + dot3(split(p[:, :B]), s_split)
        for i in range(1, ROWS):
            send_state(i).start()
        sbuf_ref[my_h] = sout_ref[z]

    for h in range(2):

        @pl.when(z != owner_z(h))
        def _():
            pltpu.make_async_remote_copy(
                src_ref=sout_ref.at[0], dst_ref=sbuf_ref.at[h],
                send_sem=s_send.at[0], recv_sem=s_recv.at[h],
                device_id=at_z(owner_z(h)), device_id_type=MESH,
            ).wait_recv()

    squares = [None] * NB
    for h in range(2):
        sh, sl = split(sbuf_ref[h])
        shh = jnp.concatenate([sh, sh], 0)
        for b in range(NB):
            rows = pl.ds(b * B, B)
            qp = qp_ref[h, rows]
            o = o1_ref[h, rows] + dotf(qp, shh) + dotf(qp[:, :B], sl)
            o1_ref[h, rows] = o
            squares[b] = o * o if h == 0 else squares[b] + o * o
    ones = jnp.ones((8, B), BF16)
    sub = iota((8, B), 0)
    sums = jnp.zeros((8, B), F32)
    for b in range(NB):
        hi, lo = split(squares[b])
        sums = jnp.where(sub == b, dot_nt(ones, hi) + dot_nt(ones, lo), sums)
    xsend_ref[...] = sums

    def send_x(i):
        return pltpu.make_async_remote_copy(
            src_ref=xsend_ref, dst_ref=xbuf_ref.at[i - 1],
            send_sem=x_send.at[i - 1], recv_sem=x_recv.at[i - 1],
            device_id={"head": lax.rem(head + i, 8)}, device_id_type=MESH,
        )

    for i in range(1, 8):
        send_x(i).start()
    for i in range(1, 8):
        send_x(i).wait()
        sums = sums + xbuf_ref[i - 1]
    scale = lax.rsqrt(sums / WIDTH + EPS)
    start_ref[...] = jnp.concatenate([scale] * 16, 0).T
    for h in range(2):
        gain = gain_ref[:, h * B : h * B + B]
        for b in range(NB):
            rows = pl.ds(b * B, B)
            o_ref[rows, h * B : h * B + B] = (
                o1_ref[h, rows] * start_ref[:, b : b + 1] * gain
            ).astype(BF16)

    for h in range(2):

        @pl.when(z != owner_z(h))
        def _():
            send_map(h, 0).wait_send()
            send_map(h, 1).wait_send()

    @pl.when(mine)
    def _():
        for i in range(1, ROWS):
            send_state(i).wait_send()


def local(queries, key_vectors, value_vectors, write_rates, doc_lengths, norm_gain):
    vm = pl.BlockSpec(memory_space=pltpu.VMEM)
    return pl.pallas_call(
        kernel,
        out_shape=jax.ShapeDtypeStruct(queries.shape, BF16),
        in_specs=[pl.BlockSpec(memory_space=pltpu.SMEM)] + [vm] * 5,
        out_specs=vm,
        scratch_shapes=[
            pltpu.VMEM((B, B), F32),
            pltpu.VMEM((2, NB, B, 2 * B), F32),
            pltpu.VMEM((2, NB, B, 2 * B), F32),
            pltpu.VMEM((2, 5, B, 2 * B), F32),
            pltpu.VMEM((2, 2, B, B), F32),
            pltpu.VMEM((ROWS, 2, B, B), F32),
            pltpu.VMEM((3, B, B), F32),
            pltpu.VMEM((2, B, B), F32),
            pltpu.VMEM((ROWS, B, 2 * B), F32),
            pltpu.VMEM((ROWS, B, B), F32),
            pltpu.VMEM((2, B, B), F32),
            pltpu.VMEM((2, NB * B, 2 * B), BF16),
            pltpu.VMEM((2, NB * B, B), F32),
            pltpu.VMEM((8, B), F32),
            pltpu.VMEM((7, 8, B), F32),
            pltpu.SemaphoreType.DMA((2, 2)),
            pltpu.SemaphoreType.DMA((ROWS, 2)),
            pltpu.SemaphoreType.DMA((3,)),
            pltpu.SemaphoreType.DMA((3,)),
            pltpu.SemaphoreType.DMA((ROWS,)),
            pltpu.SemaphoreType.DMA((2,)),
            pltpu.SemaphoreType.DMA((7,)),
            pltpu.SemaphoreType.DMA((7,)),
        ],
        compiler_params=pltpu.CompilerParams(
            collective_id=0, has_side_effects=True, vmem_limit_bytes=48 << 20
        ),
    )(doc_lengths, queries, key_vectors, value_vectors, write_rates, norm_gain[None])


def solution(mesh):
    tokens = P("ctx", "head")
    return jax.shard_map(
        local, mesh=mesh, in_specs=(tokens,) * 4 + (P(), P("head")), out_specs=tokens,
        check_vma=False,
    )
```

time: 492 us -> 52.3 us (0.11)
  the two profiles are of different devices: /device:TPU:249 before, /device:TPU:1 now
where the time goes in v1:
time: 52.3 us; the launch traced here: 52.1 us
  Pallas kernels  48.2 us (92%)
  local copies, waits for them, and re-layouts  3.93 us (8%)
    pallas_call x1, Pallas kernels, local(): pl.pallas_call(kernel, out_shape=jax.ShapeDtypeStruct(queries.shape, BF16...  48.2 us
    unnamed x12, local copies, waits for them, and re-layouts  3.93 us

profile of v1, /device:TPU:1, one launch (start us, length us, event | category | flops | bytes accessed | tf_op | source)
XLA Modules:
  0.0 52.1 jit_solution(15374525006085300145)
XLA Ops:
  0.0 0.0 copy-start
  0.0 0.0 copy-start.3
  0.0 0.0 copy-start.4
  0.0 1.0 %copy.7.rate_ref = f32[1024,2]{1,0:T(8,128)S(1)} copy(f32[1024,2]{0,1:T(2,128)} %param.9) | data formatting | bytes 16384 | tf_op args[3]
  1.0 0.1 copy-done
  1.1 0.0 copy-done.3
  1.1 0.0 copy-done.4
  1.1 0.0 copy-start.1
  1.1 1.0 %copy-done.1 = bf16[1024,256]{1,0:T(8,128)(2,1)S(1)} copy-done((bf16[1024,256]{1,0:T(8,128)(2,1)S(1)}, bf16[1024,256]{1,0:T(8,128)(2,1)}, u32[]{:S(2)}) %copy-start.1) | copy-done | bytes 524312
  2.1 0.0 copy-start.2
  2.1 1.0 %copy-done.2 = bf16[1024,256]{1,0:T(8,128)(2,1)S(1)} copy-done((bf16[1024,256]{1,0:T(8,128)(2,1)S(1)}, bf16[1024,256]{1,0:T(8,128)(2,1)}, u32[]{:S(2)}) %copy-start.2) | copy-done | bytes 524312
  3.1 48.2 %shard_map.64 = bf16[1024,256]{1,0:T(8,128)(2,1)S(1)} custom-call(s32[32]{0:T(128)S(1)} %copy-done.4, bf16[1024,256]{1,0:T(8,128)(2,1)S(1)} %copy-done, bf16[1024,256]{1,0:T(8,128)(2,1)S(1)} %copy-done.1, bf16[1024,256]{1,0:T(8,128)(2,1)S(1)} %copy-done.2, f32[1024,2]{1,0:T(8,128)S(1)} %copy.7.rate_ref, f32[1,256]{1,0:T(1,128)S(1)} %bitcast.1), custom_call_target="tpu_custom_call" | custom-call | tf_op jit(solution)/shard_map/pallas_call | solution.py:349
  51.3 0.8 %copy.9 = bf16[1024,256]{1,0:T(8,128)(2,1)} copy(bf16[1024,256]{1,0:T(8,128)(2,1)S(1)} %shard_map.64) | data formatting | bytes 1048576
Async XLA Ops:
  0.0 1.1 %copy-start = (bf16[1024,256]{1,0:T(8,128)(2,1)S(1)}, bf16[1024,256]{1,0:T(8,128)(2,1)}, u32[]{:S(2)}) copy-start(bf16[1024,256]{1,0:T(8,128)(2,1)} %q_ref.1) | copy-start | bytes 1572868
  0.0 1.1 %copy-start.3 = (f32[256]{0:T(256)S(1)}, f32[256]{0:T(256)}, u32[]{:S(2)}) copy-start(f32[256]{0:T(256)} %param.11) | copy-start | bytes 3076
  0.0 1.1 %copy-start.4 = (s32[32]{0:T(128)S(1)}, s32[32]{0:T(128)}, u32[]{:S(2)}) copy-start(s32[32]{0:T(128)} %doc_ref.1) | copy-start | bytes 388
  1.1 1.0 %copy-start.1 = (bf16[1024,256]{1,0:T(8,128)(2,1)S(1)}, bf16[1024,256]{1,0:T(8,128)(2,1)}, u32[]{:S(2)}) copy-start(bf16[1024,256]{1,0:T(8,128)(2,1)} %k_ref.1) | copy-start | bytes 1572868
  2.1 1.0 %copy-start.2 = (bf16[1024,256]{1,0:T(8,128)(2,1)S(1)}, bf16[1024,256]{1,0:T(8,128)(2,1)}, u32[]{:S(2)}) copy-start(bf16[1024,256]{1,0:T(8,128)(2,1)} %v_ref.1) | copy-start | bytes 1572868

commit v2 on v1

--- a/solution.py
+++ b/solution.py
@@ -47,40 +47,58 @@
     return lax.broadcasted_iota(jnp.int32, shape, dim)
 
 
+SIZES = (8, 16, 32, 64)
+
+
+def stack_parts(x):
+    hi = x.astype(BF16).astype(F32)
+    return jnp.concatenate([hi, x - hi], 0).astype(BF16)
+
+
+def dot_stacked(a, b):
+    m, n = a.shape[0] // 2, b.shape[1] // 2
+    r = dotf(a, b)
+    return r[:m, :n] + (r[m:, :n] + r[:m, n:])
+
+
 def invert(lows):
     row, col = iota((B, B), 0), iota((B, B), 1)
+    n = len(lows)
     near = (row // 8) == (col // 8)
-    n = len(lows)
-    parts = []
-    for low in lows:
-        c = jnp.sum(jnp.where(near, low, 0.0).reshape(16, 8, B), axis=0)
-        hi = c.astype(BF16).astype(F32)
-        parts += [hi, c - hi]
-    stacked = jnp.concatenate(parts, 0).astype(BF16)
+    parts = [
+        stack_parts(jnp.sum(jnp.where(near, low, 0.0).reshape(16, 8, B), axis=0)) for low in lows
+    ]
+    lsp = [jnp.concatenate(split(low), 1) for low in lows]
+    stacked = jnp.concatenate(parts, 0)
     spread = []
     for m in range(7):
         pick = jnp.where(near & (row % 8 == m), 1.0, 0.0).astype(BF16)
-        spread.append(dotf(stacked, pick))
-    eye8 = (iota((8, B), 1) % 8 == iota((8, B), 0)).astype(F32)
-    inv = []
-    for s in range(n):
-        t = eye8
-        for m in range(7):
-            coef = spread[m][16 * s : 16 * s + 8] + spread[m][16 * s + 8 : 16 * s + 16]
-            t = t - coef * t[m : m + 1]
-        inv.append(jnp.where(near, jnp.concatenate([t] * 16, 0), 0.0))
-    lsp = [split(low) for low in lows]
-    for size in (8, 16, 32, 64):
-        r, c = iota((64, B), 0), iota((64, B), 1)
-        keep = (c // size) == 2 * (r // size)
+        r = dotf(stacked, pick).reshape(n, 2, 8, B)
+        spread.append(r[:, 0] + r[:, 1])
+    inv = jnp.broadcast_to((iota((8, B), 1) % 8 == iota((8, B), 0)).astype(F32), (n, 8, B))
+    for m in range(7):
+        inv = inv - spread[m] * inv[:, m : m + 1]
+    inv = [inv[s] for s in range(n)]
+    row2, col2 = iota((B, 2 * B), 0), iota((B, 2 * B), 1) % B
+    for size in SIZES:
+        below = (row2 // size == col2 // size + 1) & (row2 // size % 2 == 1)
+        same = row2 // size == col2 // size
+        odd = iota((size, B), 1) // size % 2 == 1
+        xs, tops = [], []
         for s in range(n):
-            t4 = inv[s].reshape(64 // size, 2, size, B)
-            even, odd = t4[:, 0], t4[:, 1].reshape(64, B)
-            x = jnp.where(keep, dot3(split(odd), lsp[s]), 0.0)
-            odd = odd - dot3(split(x), split(inv[s]))
-            inv[s] = jnp.concatenate(
-                [even[:, None], odd.reshape(64 // size, 1, size, B)], 1
-            ).reshape(B, B)
+            upper = jnp.where(odd, 0.0, inv[s])
+            inv[s] = jnp.where(odd, inv[s], 0.0)
+            tops.append(upper)
+            low = jnp.where(below, lsp[s], jnp.zeros_like(lsp[s]))
+            xs.append(dot_stacked(stack_parts(inv[s]), low))
+        for s in range(n):
+            two = [tops[s]] * (16 // size if size < 16 else 1)
+            two = jnp.concatenate(two, 0) if len(two) > 1 else two[0]
+            wide = jnp.concatenate(split(two), 1)
+            wide = jnp.concatenate([wide] * (B // wide.shape[0]), 0)
+            wide = jnp.where(same, wide, jnp.zeros_like(wide))
+            y = dot_stacked(stack_parts(xs[s]), wide)
+            inv[s] = jnp.concatenate([tops[s], inv[s] - y], 0)
     return inv
 
 
@@ -155,15 +173,16 @@
             lows.append(jnp.where(keep, dot_nt(kb, kb) * (scale * rk), 0.0))
             rights.append(split(jnp.concatenate([kf * (scale * rk), vf * scale], 1)))
         inv = invert(lows)
-        maps = []
-        for b in range(NB):
-            wu = dot3(split(inv[b]), rights[b])
+        maps, wus = [], []
+        for b in range(NB):
+            wus.append(dot3(split(inv[b]), rights[b]))
+        for b in range(NB):
             _, carry, last = doc_columns(b)
-            w, u = wu[:, :B] * carry, wu[:, B:]
+            w, u = wus[b][:, :B] * carry, wus[b][:, B:]
             wu_ref[h, b] = jnp.concatenate([w, u], 1)
             hi, lo = split(jnp.concatenate([w * last, u * last], 1))
-            kb = k_ref[pl.ds(b * B, B), lanes(h)]
-            ma = dot_tn(jnp.concatenate([kb, kb], 0), jnp.concatenate([hi, lo], 0))
+            kt = k_ref[pl.ds(b * B, B), lanes(h)].T
+            ma = dotf(jnp.concatenate([kt, kt], 1), jnp.concatenate([hi, lo], 0))
             m = jnp.where(row == col, carry[B - 1 : B], 0.0) - ma[:, :B]
             maps.append(jnp.concatenate([m, ma[:, B:]], 1))
             map_ref[h, b] = maps[b]
@@ -204,7 +223,7 @@
         pre[3] = combine(map_ref[h, 2], pre[2])
         pre[5] = combine(map_ref[h, 4], pre[4])
         pre[6] = combine(pre_ref[h, 4], pre[4])
-        pre[7] = combine(map_ref[h, 6], pre[6])
+        scores, lefts = [], []
         for b in range(NB):
             kb = k_ref[pl.ds(b * B, B), lanes(h)]
             qb = q_ref[pl.ds(b * B, B), lanes(h)]
@@ -212,14 +231,17 @@
             rq = lax.rsqrt(jnp.sum(qf * qf, axis=1, keepdims=True) + EPS)
             first, carry, _ = doc_columns(b)
             keep = (row >= col) & (colf + float(b * B) >= first)
-            sc = jnp.where(keep, dot_nt(qb, kb) * rq, 0.0)
-            swu = dot3(split(sc), split(wu_ref[h, b]))
-            qe = qf * (rq * carry) - swu[:, :B]
-            o1 = swu[:, B:]
+            scores.append(jnp.where(keep, dot_nt(qb, kb) * rq, 0.0))
+            lefts.append(qf * (rq * carry))
+        pre[7] = combine(map_ref[h, 6], pre[6])
+        both = [dot3(split(scores[b]), split(wu_ref[h, b])) for b in range(NB)]
+        qes = [lefts[b] - both[b][:, :B] for b in range(NB)]
+        o1s = [both[b][:, B:] for b in range(NB)]
+        qxs = [dot3(split(qes[b]), split(pre[b])) for b in range(1, NB)]
+        for b in range(NB):
+            qe, o1 = qes[b], o1s[b]
             if b > 0:
-                qx = dot3(split(qe), split(pre[b]))
-                qe = qx[:, :B]
-                o1 = o1 + qx[:, B:]
+                qe, o1 = qxs[b - 1][:, :B], o1 + qxs[b - 1][:, B:]
             hi, lo = split(qe)
             qp_ref[h, pl.ds(b * B, B)] = jnp.concatenate([hi, lo], 1)
             o1_ref[h, pl.ds(b * B, B)] = o1

time: 52.3 us -> 44.9 us (0.86)
  Pallas kernels: 48.2 us -> 40.8 us
    pallas_call x1, Pallas kernels: 48.2 us -> 40.8 us  [local(): pl.pallas_call(kernel, out_shape=jax.ShapeDtypeStruct(queries.shape, BF16...]
where the time goes in v2:
time: 44.9 us; the launch traced here: 44.8 us
  Pallas kernels  40.8 us (91%)
  local copies, waits for them, and re-layouts  3.93 us (9%)
    pallas_call x1, Pallas kernels, local(): pl.pallas_call(kernel, out_shape=jax.ShapeDtypeStruct(queries.shape, BF16...  40.8 us
    unnamed x12, local copies, waits for them, and re-layouts  3.93 us

profile of v2, /device:TPU:1, one launch (start us, length us, event | category | flops | bytes accessed | tf_op | source)
XLA Modules:
  0.0 44.8 jit_solution(4078670867888355456)
XLA Ops:
  0.0 0.0 copy-start
  0.0 0.0 copy-start.3
  0.0 0.0 copy-start.4
  0.0 1.0 %copy.7.rate_ref = f32[1024,2]{1,0:T(8,128)S(1)} copy(f32[1024,2]{0,1:T(2,128)} %param.9) | data formatting | bytes 16384 | tf_op args[3]
  1.0 0.1 copy-done
  1.1 0.0 copy-done.3
  1.1 0.0 copy-done.4
  1.1 0.0 copy-start.1
  1.1 1.0 %copy-done.1 = bf16[1024,256]{1,0:T(8,128)(2,1)S(1)} copy-done((bf16[1024,256]{1,0:T(8,128)(2,1)S(1)}, bf16[1024,256]{1,0:T(8,128)(2,1)}, u32[]{:S(2)}) %copy-start.1) | copy-done | bytes 524312
  2.1 0.0 copy-start.2
  2.1 1.0 %copy-done.2 = bf16[1024,256]{1,0:T(8,128)(2,1)S(1)} copy-done((bf16[1024,256]{1,0:T(8,128)(2,1)S(1)}, bf16[1024,256]{1,0:T(8,128)(2,1)}, u32[]{:S(2)}) %copy-start.2) | copy-done | bytes 524312
  3.1 40.8 %shard_map.64 = bf16[1024,256]{1,0:T(8,128)(2,1)S(1)} custom-call(s32[32]{0:T(128)S(1)} %copy-done.4, bf16[1024,256]{1,0:T(8,128)(2,1)S(1)} %copy-done, bf16[1024,256]{1,0:T(8,128)(2,1)S(1)} %copy-done.1, bf16[1024,256]{1,0:T(8,128)(2,1)S(1)} %copy-done.2, f32[1024,2]{1,0:T(8,128)S(1)} %copy.7.rate_ref, f32[1,256]{1,0:T(1,128)S(1)} %bitcast.1), custom_call_target="tpu_custom_call" | custom-call | tf_op jit(solution)/shard_map/pallas_call | solution.py:371
  44.0 0.8 %copy.9 = bf16[1024,256]{1,0:T(8,128)(2,1)} copy(bf16[1024,256]{1,0:T(8,128)(2,1)S(1)} %shard_map.64) | data formatting | bytes 1048576
Async XLA Ops:
  0.0 1.1 %copy-start = (bf16[1024,256]{1,0:T(8,128)(2,1)S(1)}, bf16[1024,256]{1,0:T(8,128)(2,1)}, u32[]{:S(2)}) copy-start(bf16[1024,256]{1,0:T(8,128)(2,1)} %q_ref.1) | copy-start | bytes 1572868
  0.0 1.1 %copy-start.3 = (f32[256]{0:T(256)S(1)}, f32[256]{0:T(256)}, u32[]{:S(2)}) copy-start(f32[256]{0:T(256)} %param.11) | copy-start | bytes 3076
  0.0 1.1 %copy-start.4 = (s32[32]{0:T(128)S(1)}, s32[32]{0:T(128)}, u32[]{:S(2)}) copy-start(s32[32]{0:T(128)} %doc_ref.1) | copy-start | bytes 388
  1.1 1.0 %copy-start.1 = (bf16[1024,256]{1,0:T(8,128)(2,1)S(1)}, bf16[1024,256]{1,0:T(8,128)(2,1)}, u32[]{:S(2)}) copy-start(bf16[1024,256]{1,0:T(8,128)(2,1)} %k_ref.1) | copy-start | bytes 1572868
  2.1 1.0 %copy-start.2 = (bf16[1024,256]{1,0:T(8,128)(2,1)S(1)}, bf16[1024,256]{1,0:T(8,128)(2,1)}, u32[]{:S(2)}) copy-start(bf16[1024,256]{1,0:T(8,128)(2,1)} %v_ref.1) | copy-start | bytes 1572868

commit v3 on v2

--- a/solution.py
+++ b/solution.py
@@ -103,11 +103,27 @@
 
 
 def kernel(
-    doc_ref, q_ref, k_ref, v_ref, rate_ref, gain_ref, o_ref,
-    start_ref, wu_ref, map_ref, pre_ref, mat_ref, got_ref, ybuf_ref, ysend_ref, pz_ref,
+    doc_ref, q_hbm, k_hbm, v_hbm, rate_hbm, gain_hbm, o_ref,
+    q_ref, k_ref, v_ref, rate_ref, gain_ref, cols_ref, scale_ref, wu_ref, map_ref, pre_ref, mat_ref, got_ref, ybuf_ref, ysend_ref, pm_ref, pa_ref,
     sout_ref, sbuf_ref, qp_ref, o1_ref, xsend_ref, xbuf_ref,
-    g_send, g_recv, y_send, y_recv, s_send, s_recv, x_send, x_recv,
+    in_sem, g_send, g_recv, y_send, y_recv, s_send, s_recv, x_send, x_recv,
 ):
+    def load(i, hbm, ref, h):
+        if h is not None:
+            hbm, ref = hbm.at[:, h * B : h * B + B], ref.at[:, h * B : h * B + B]
+        return pltpu.make_async_copy(hbm, ref, in_sem.at[i])
+
+    loads = [
+        load(0, rate_hbm, rate_ref, None),
+        load(1, k_hbm, k_ref, 0),
+        load(2, v_hbm, v_ref, 0),
+        load(3, k_hbm, k_ref, 1),
+        load(4, v_hbm, v_ref, 1),
+        load(5, gain_hbm, gain_ref, None),
+        load(6, q_hbm, q_ref, None),
+    ]
+    for copy in loads:
+        copy.start()
     ctx, head = lax.axis_index("ctx"), lax.axis_index("head")
     y, z = ctx // ROWS, lax.rem(ctx, ROWS)
     core = lax.rem(head, 2)
@@ -139,15 +155,18 @@
     for m in range(31):
         begin = begin + doc_ref[m]
         start = jnp.where(pos >= begin, begin, start)
+    loads[0].wait()
+    rates = [rate_ref[h : h + 1, b * B : b * B + B] for h in range(2) for b in range(NB)]
     start_f = (start - base).astype(F32)
-    start_ref[...] = jnp.concatenate([start_f] * 16, 0).T
+    cols_ref[...] = jnp.concatenate([start_f] + rates + [start_f] * 13, 0).T
 
     row, col = iota((B, B), 0), iota((B, B), 1)
+    eye = (row == col).astype(F32)
     row1 = iota((B, 1), 0).astype(F32)
     colf = col.astype(F32)
 
     def doc_columns(b):
-        first = start_ref[:, b : b + 1]
+        first = cols_ref[:, b : b + 1]
         carry = (first < float(b * B)).astype(F32)
         last = (row1 + float(b * B) >= first[B - 1 : B]).astype(F32)
         return first, carry, last
@@ -156,8 +175,8 @@
         return pl.ds(pl.multiple_of(h * B, B), B)
 
     def rate(b, h):
-        r = rate_ref[pl.ds(b * B, B), :]
-        return jnp.where(h == 0, r[:, 0:1], r[:, 1:2])
+        i = NB + h * NB + b
+        return cols_ref[:, i : i + 1]
 
     def own_map(h):
         lows, rights = [], []
@@ -205,6 +224,8 @@
         )
 
     for h in range(2):
+        loads[1 + 2 * h].wait()
+        loads[2 + 2 * h].wait()
         own_map(h)
         if h == 0:
             pl.semaphore_wait(barrier, 17)
@@ -246,6 +267,8 @@
             qp_ref[h, pl.ds(b * B, B)] = jnp.concatenate([hi, lo], 1)
             o1_ref[h, pl.ds(b * B, B)] = o1
 
+    loads[5].wait()
+    loads[6].wait()
     for h in range(2):
         shadow(h)
 
@@ -289,18 +312,21 @@
         pre[5] = combine(maps[4], pre[4])
         pre[6] = combine(pairs[2], pre[4])
         pre[7] = combine(maps[6], pre[6])
-        for i in range(1, ROWS):
-            pz_ref[i] = pre[i]
+        for i in range(ROWS):
+            p = pre[i] if i else jnp.concatenate([eye, jnp.zeros_like(eye)], 1)
+            pm_ref[i] = jnp.concatenate(split(p[:, :B]), 1)
+            pa_ref[i] = p[:, B:]
         for c in sends:
             c.wait()
         s_row = ybuf_ref[1] + dot3(split(ybuf_ref[0]), split(ybuf_ref[2]))
-        sout_ref[0] = s_row
-        s_split = split(s_row)
-        for i in range(1, ROWS):
-            p = pz_ref[i]
-            sout_ref[i] = p[:, B:] + dot3(split(p[:, :B]), s_split)
-        for i in range(1, ROWS):
-            send_state(i).start()
+        sh, sl = split(s_row)
+        shh = jnp.concatenate([sh, sh], 0)
+        for i in (4, 3, 5, 2, 6, 1, 7, 0):
+            to = lax.rem(z + i, ROWS)
+            pm = pm_ref[to]
+            sout_ref[to] = pa_ref[to] + dotf(pm, shh) + dotf(pm[:, :B], sl)
+            if i:
+                send_state(i).start()
         sbuf_ref[my_h] = sout_ref[z]
 
     for h in range(2):
@@ -344,13 +370,13 @@
         send_x(i).wait()
         sums = sums + xbuf_ref[i - 1]
     scale = lax.rsqrt(sums / WIDTH + EPS)
-    start_ref[...] = jnp.concatenate([scale] * 16, 0).T
+    scale_ref[...] = jnp.concatenate([scale] * 16, 0).T
     for h in range(2):
         gain = gain_ref[:, h * B : h * B + B]
         for b in range(NB):
             rows = pl.ds(b * B, B)
             o_ref[rows, h * B : h * B + B] = (
-                o1_ref[h, rows] * start_ref[:, b : b + 1] * gain
+                o1_ref[h, rows] * scale_ref[:, b : b + 1] * gain
             ).astype(BF16)
 
     for h in range(2):
@@ -370,10 +396,17 @@
     vm = pl.BlockSpec(memory_space=pltpu.VMEM)
     return pl.pallas_call(
         kernel,
-        out_shape=jax.ShapeDtypeStruct(queries.shape, BF16),
-        in_specs=[pl.BlockSpec(memory_space=pltpu.SMEM)] + [vm] * 5,
+        out_shape=pltpu.VMEM(queries.shape, BF16),
+        in_specs=[pl.BlockSpec(memory_space=pltpu.SMEM)]
+        + [pl.BlockSpec(memory_space=pltpu.HBM)] * 5,
         out_specs=vm,
         scratch_shapes=[
+            pltpu.VMEM((NB * B, 2 * B), BF16),
+            pltpu.VMEM((NB * B, 2 * B), BF16),
+            pltpu.VMEM((NB * B, 2 * B), BF16),
+            pltpu.VMEM((2, NB * B), F32),
+            pltpu.VMEM((1, 2 * B), F32),
+            pltpu.VMEM((B, B), F32),
             pltpu.VMEM((B, B), F32),
             pltpu.VMEM((2, NB, B, 2 * B), F32),
             pltpu.VMEM((2, NB, B, 2 * B), F32),
@@ -382,13 +415,15 @@
             pltpu.VMEM((ROWS, 2, B, B), F32),
             pltpu.VMEM((3, B, B), F32),
             pltpu.VMEM((2, B, B), F32),
-            pltpu.VMEM((ROWS, B, 2 * B), F32),
+            pltpu.VMEM((ROWS, B, 2 * B), BF16),
+            pltpu.VMEM((ROWS, B, B), F32),
             pltpu.VMEM((ROWS, B, B), F32),
             pltpu.VMEM((2, B, B), F32),
             pltpu.VMEM((2, NB * B, 2 * B), BF16),
             pltpu.VMEM((2, NB * B, B), F32),
             pltpu.VMEM((8, B), F32),
             pltpu.VMEM((7, 8, B), F32),
+            pltpu.SemaphoreType.DMA((7,)),
             pltpu.SemaphoreType.DMA((2, 2)),
             pltpu.SemaphoreType.DMA((ROWS, 2)),
             pltpu.SemaphoreType.DMA((3,)),
@@ -399,9 +434,9 @@
             pltpu.SemaphoreType.DMA((7,)),
         ],
         compiler_params=pltpu.CompilerParams(
-            collective_id=0, has_side_effects=True, vmem_limit_bytes=48 << 20
+            collective_id=0, has_side_effects=True, vmem_limit_bytes=63 << 20
         ),
-    )(doc_lengths, queries, key_vectors, value_vectors, write_rates, norm_gain[None])
+    )(doc_lengths, queries, key_vectors, value_vectors, write_rates.T, norm_gain[None])
 
 
 def solution(mesh):

time: 44.9 us -> 42.8 us (0.953)
  local copies, waits for them, and re-layouts: 3.93 us -> 0.8 us
  Pallas kernels: 40.8 us -> 41.9 us
    unnamed x12 -> x1, local copies, waits for them, and re-layouts: 3.93 us -> 0.8 us
    pallas_call x1, Pallas kernels: 40.8 us -> 41.9 us  [local(): pl.pallas_call(kernel, out_shape=pltpu.VMEM(queries.shape, BF16), in_spec...]
where the time goes in v3:
time: 42.8 us; the launch traced here: 42.7 us
  Pallas kernels  41.9 us (98%)
  local copies, waits for them, and re-layouts  0.8 us (2%)
    pallas_call x1, Pallas kernels, local(): pl.pallas_call(kernel, out_shape=pltpu.VMEM(queries.shape, BF16), in_spec...  41.9 us

profile of v3, /device:TPU:1, one launch (start us, length us, event | category | flops | bytes accessed | tf_op | source)
XLA Modules:
  0.0 42.7 jit_solution(10443245407904786946)
XLA Ops:
  0.0 41.9 %shard_map.64 = bf16[1024,256]{1,0:T(8,128)(2,1)S(1)} custom-call(s32[32]{0:T(128)} %doc_ref.1, bf16[1024,256]{1,0:T(8,128)(2,1)} %q_hbm.1, bf16[1024,256]{1,0:T(8,128)(2,1)} %k_hbm.1, bf16[1024,256]{1,0:T(8,128)(2,1)} %v_hbm.1, f32[2,1024]{1,0:T(2,128)} %bitcast.2, f32[1,256]{1,0:T(1,128)} %bitcast.3), custom_call_target="tpu_custom_call" | custom-call | tf_op jit(solution)/shard_map/pallas_call | solution.py:397
  41.9 0.8 %copy.8 = bf16[1024,256]{1,0:T(8,128)(2,1)} copy(bf16[1024,256]{1,0:T(8,128)(2,1)S(1)} %shard_map.64) | data formatting | bytes 1048576

commit v4 on v3

--- a/solution.py
+++ b/solution.py
@@ -38,9 +38,63 @@
     return dotf(jnp.concatenate([ah, al], 1), jnp.concatenate([bh, bh], 0)) + dotf(ah, bl)
 
 
-def combine(later, earlier):
-    out = dot3(split(later[:, :B]), split(earlier))
-    return jnp.concatenate([out[:, :B], out[:, B:] + later[:, B:]], 1)
+def wide(x):
+    return jnp.concatenate(split(x), 1)
+
+
+def dotw(a, b):
+    n = b.shape[1] // 2
+    r = dotf(a, jnp.concatenate([b, b], 0))
+    return r[:, :n] + r[:, n:]
+
+
+def products(ms):
+    w = [wide(m) for m in ms]
+    m01, m23, m45, m67 = [dotw(w[i + 1], w[i]) for i in range(0, 8, 2)]
+    w01, w23, w45, w67 = [wide(m) for m in (m01, m23, m45, m67)]
+    m03, m47 = dotw(w23, w01), dotw(w67, w45)
+    w03, w47 = wide(m03), wide(m47)
+    total = dotw(w47, w03)
+    w27 = wide(dotw(w47, w23))
+    after = [dotw(w27, w[1]), None, dotw(w47, w[3]), None, dotw(w67, w[5])]
+    after = [wide(after[0]), w27, wide(after[2]), w47, wide(after[4]), w67, w[7]]
+    return total, after, (w, w01, w23, w45, w03)
+
+
+def before(ws):
+    w, w01, w23, w45, w03 = ws
+    w6 = wide(dotw(w45, w03))
+    return [w[0], w01, wide(dotw(w[2], w01)), w03, wide(dotw(w[4], w03)), w6, wide(dotw(w[6], w6))]
+
+
+def added(a, get):
+    a01 = dotw(get("1"), wide(a[0])) + a[1]
+    a23 = dotw(get("3"), wide(a[2])) + a[3]
+    a45 = dotw(get("5"), wide(a[4])) + a[5]
+    w01 = wide(a01)
+    a03 = dotw(get("23"), w01) + a23
+    w03 = wide(a03)
+    a6 = dotw(get("45"), w03) + a45
+    return [
+        a[0], a01, dotw(get("2"), w01) + a[2], a03, dotw(get("4"), w03) + a[4], a6,
+        dotw(get("6"), wide(a6)) + a[6],
+    ]
+
+
+def total_added(after, a):
+    t = a[7]
+    for i in range(7):
+        t = t + dotw(after[i], wide(a[i]))
+    return t
+
+
+NAMES = {"1": 0, "2": 1, "3": 2, "4": 3, "5": 4, "6": 5, "23": 6, "45": 7}
+
+
+def keep_products(ref, ws):
+    w, w01, w23, w45, w03 = ws
+    for name, x in zip(NAMES, [w[1], w[2], w[3], w[4], w[5], w[6], w23, w45]):
+        ref[NAMES[name]] = x
 
 
 def iota(shape, dim):
@@ -104,7 +158,7 @@
 
 def kernel(
     doc_ref, q_hbm, k_hbm, v_hbm, rate_hbm, gain_hbm, o_ref,
-    q_ref, k_ref, v_ref, rate_ref, gain_ref, cols_ref, scale_ref, wu_ref, map_ref, pre_ref, mat_ref, got_ref, ybuf_ref, ysend_ref, pm_ref, pa_ref,
+    q_ref, k_ref, v_ref, rate_ref, gain_ref, cols_ref, scale_ref, wu_ref, bm_ref, prod_ref, add_ref, mat_ref, got_ref, ybuf_ref, ysend_ref, pz_ref, pa_ref, oprod_ref, oafter_ref,
     sout_ref, sbuf_ref, qp_ref, o1_ref, xsend_ref, xbuf_ref,
     in_sem, g_send, g_recv, y_send, y_recv, s_send, s_recv, x_send, x_recv,
 ):
@@ -178,43 +232,47 @@
         i = NB + h * NB + b
         return cols_ref[:, i : i + 1]
 
-    def own_map(h):
-        lows, rights = [], []
+    def own_product(h):
+        lows, rights, scales = [], [], []
         for b in range(NB):
             kb = k_ref[pl.ds(b * B, B), lanes(h)]
             kf = kb.astype(F32)
-            vf = v_ref[pl.ds(b * B, B), lanes(h)].astype(F32)
             rk = lax.rsqrt(jnp.sum(kf * kf, axis=1, keepdims=True) + EPS)
-            beta = rate(b, h)
             first, _, _ = doc_columns(b)
             keep = (row > col) & (colf + float(b * B) >= first)
-            scale = beta * rk
+            scale = rate(b, h) * rk
+            scales.append(scale)
             lows.append(jnp.where(keep, dot_nt(kb, kb) * (scale * rk), 0.0))
-            rights.append(split(jnp.concatenate([kf * (scale * rk), vf * scale], 1)))
-        inv = invert(lows)
-        maps, wus = [], []
-        for b in range(NB):
-            wus.append(dot3(split(inv[b]), rights[b]))
+            rights.append(wide(kf * (scale * rk)))
+        inv = [wide(t) for t in invert(lows)]
+        ws = [dotw(inv[b], rights[b]) for b in range(NB)]
+        ms, kts = [], []
         for b in range(NB):
             _, carry, last = doc_columns(b)
-            w, u = wus[b][:, :B] * carry, wus[b][:, B:]
-            wu_ref[h, b] = jnp.concatenate([w, u], 1)
-            hi, lo = split(jnp.concatenate([w * last, u * last], 1))
+            w = ws[b] * carry
+            wu_ref[h, b, :, :B] = w
+            hi, lo = split(w * last)
             kt = k_ref[pl.ds(b * B, B), lanes(h)].T
-            ma = dotf(jnp.concatenate([kt, kt], 1), jnp.concatenate([hi, lo], 0))
-            m = jnp.where(row == col, carry[B - 1 : B], 0.0) - ma[:, :B]
-            maps.append(jnp.concatenate([m, ma[:, B:]], 1))
-            map_ref[h, b] = maps[b]
-        pairs = [combine(maps[i + 1], maps[i]) for i in range(0, NB, 2)]
-        p03 = combine(pairs[1], pairs[0])
-        p47 = combine(pairs[3], pairs[2])
-        total = combine(p47, p03)
-        mat_ref[h, 0] = total[:, :B]
-        mat_ref[h, 1] = total[:, B:]
-        pre_ref[h, 1] = pairs[0]
-        pre_ref[h, 3] = p03
-        pre_ref[h, 4] = pairs[2]
-
+            kts.append(jnp.concatenate([kt, kt], 1))
+            m = dotf(kts[b], jnp.concatenate([hi, lo], 0))
+            ms.append(jnp.where(row == col, carry[B - 1 : B], 0.0) - m)
+        total, after, some = products(ms)
+        mat_ref[h, 0] = total
+        return inv, scales, kts, after, some
+
+    def own_added(h, inv, scales, kts, after):
+        us = []
+        for b in range(NB):
+            vf = v_ref[pl.ds(b * B, B), lanes(h)].astype(F32)
+            us.append(dotw(inv[b], wide(vf * scales[b])))
+        adds = []
+        for b in range(NB):
+            _, _, last = doc_columns(b)
+            wu_ref[h, b, :, B:] = us[b]
+            hi, lo = split(us[b] * last)
+            adds.append(dotf(kts[b], jnp.concatenate([hi, lo], 0)))
+            add_ref[h, b] = adds[b]
+        mat_ref[h, 1] = total_added(after, adds)
 
     def send_map(h, part):
         return pltpu.make_async_remote_copy(
@@ -223,27 +281,42 @@
             device_id=at_z(owner_z(h)), device_id_type=MESH,
         )
 
+    def give(h, part):
+        @pl.when(z != owner_z(h))
+        def _():
+            send_map(h, part).start()
+
+        @pl.when(z == owner_z(h))
+        def _():
+            got_ref[z, part] = mat_ref[h, part]
+
+    @pl.when(y < 2)
+    def _():
+        ybuf_ref[0] = jnp.zeros((B, B), F32)
+        ybuf_ref[2] = jnp.zeros((B, B), F32)
+
+    @pl.when(y == 0)
+    def _():
+        ybuf_ref[1] = jnp.zeros((B, B), F32)
+
+    left = []
     for h in range(2):
         loads[1 + 2 * h].wait()
-        loads[2 + 2 * h].wait()
-        own_map(h)
+        left.append(own_product(h))
         if h == 0:
             pl.semaphore_wait(barrier, 17)
-
-        @pl.when(z != owner_z(h))
-        def _():
-            send_map(h, 0).start()
-            send_map(h, 1).start()
-
-        @pl.when(z == owner_z(h))
-        def _():
-            got_ref[z] = mat_ref[h]
+        give(h, 0)
+    for h in range(2):
+        loads[2 + 2 * h].wait()
+        own_added(h, *left[h][:4])
+        give(h, 1)
+    for h in range(2):
+        keep_products(prod_ref.at[h], left[h][4])
+        for i, x in enumerate(before(left[h][4])):
+            bm_ref[h, i] = x
 
     def shadow(h):
-        pre = [None, map_ref[h, 0], pre_ref[h, 1], None, pre_ref[h, 3], None, None, None]
-        pre[3] = combine(map_ref[h, 2], pre[2])
-        pre[5] = combine(map_ref[h, 4], pre[4])
-        pre[6] = combine(pre_ref[h, 4], pre[4])
+        adds = added([add_ref[h, b] for b in range(NB)], lambda name: prod_ref[h, NAMES[name]])
         scores, lefts = [], []
         for b in range(NB):
             kb = k_ref[pl.ds(b * B, B), lanes(h)]
@@ -254,11 +327,17 @@
             keep = (row >= col) & (colf + float(b * B) >= first)
             scores.append(jnp.where(keep, dot_nt(qb, kb) * rq, 0.0))
             lefts.append(qf * (rq * carry))
-        pre[7] = combine(map_ref[h, 6], pre[6])
         both = [dot3(split(scores[b]), split(wu_ref[h, b])) for b in range(NB)]
         qes = [lefts[b] - both[b][:, :B] for b in range(NB)]
         o1s = [both[b][:, B:] for b in range(NB)]
-        qxs = [dot3(split(qes[b]), split(pre[b])) for b in range(1, NB)]
+        qxs = []
+        for b in range(1, NB):
+            bm, (ah, al) = bm_ref[h, b - 1], split(adds[b - 1])
+            right = (
+                jnp.concatenate([bm[:, :B], ah], 1),
+                jnp.concatenate([bm[:, B:], al], 1),
+            )
+            qxs.append(dot3(split(qes[b]), right))
         for b in range(NB):
             qe, o1 = qes[b], o1s[b]
             if b > 0:
@@ -287,43 +366,59 @@
             device_id=at_z(to), device_id_type=MESH,
         )
 
+    def wait_maps(part):
+        for i in range(1, ROWS):
+            frm = lax.rem(z + i, ROWS)
+            pltpu.make_async_remote_copy(
+                src_ref=mat_ref.at[0, part], dst_ref=got_ref.at[frm, part],
+                send_sem=g_send.at[0, part], recv_sem=g_recv.at[frm, part],
+                device_id=at_z(frm), device_id_type=MESH,
+            ).wait_recv()
+
     @pl.when(mine)
     def _():
-        for i in range(1, ROWS):
-            frm = lax.rem(z + i, ROWS)
-            for part in range(2):
-                pltpu.make_async_remote_copy(
-                    src_ref=mat_ref.at[0, part], dst_ref=got_ref.at[frm, part],
-                    send_sem=g_send.at[0, part], recv_sem=g_recv.at[frm, part],
-                    device_id=at_z(frm), device_id_type=MESH,
-                ).wait_recv()
-        maps = [jnp.concatenate([got_ref[i, 0], got_ref[i, 1]], 1) for i in range(ROWS)]
-        pairs = [combine(maps[i + 1], maps[i]) for i in range(0, ROWS, 2)]
-        p03 = combine(pairs[1], pairs[0])
-        p47 = combine(pairs[3], pairs[2])
-        total = combine(p47, p03)
-        ysend_ref[0] = total[:, :B]
-        ysend_ref[1] = total[:, B:]
-        sends = [send_y(0, 0, 1), send_y(1, 1, 1), send_y(1, 2, 2)]
-        for c in sends:
-            c.start()
-        pre = [None, maps[0], pairs[0], None, p03, None, None, None]
-        pre[3] = combine(maps[2], pre[2])
-        pre[5] = combine(maps[4], pre[4])
-        pre[6] = combine(pairs[2], pre[4])
-        pre[7] = combine(maps[6], pre[6])
-        for i in range(ROWS):
-            p = pre[i] if i else jnp.concatenate([eye, jnp.zeros_like(eye)], 1)
-            pm_ref[i] = jnp.concatenate(split(p[:, :B]), 1)
-            pa_ref[i] = p[:, B:]
-        for c in sends:
-            c.wait()
-        s_row = ybuf_ref[1] + dot3(split(ybuf_ref[0]), split(ybuf_ref[2]))
+        wait_maps(0)
+        total, after, some = products([got_ref[i, 0] for i in range(ROWS)])
+        ysend_ref[0] = total
+        @pl.when((y == 1) | (y == 2))
+        def _():
+            send_y(0, 0, 1).start()
+
+        keep_products(oprod_ref, some)
+        pz_ref[0] = jnp.concatenate([eye, jnp.zeros_like(eye)], 1).astype(BF16)
+        for i, x in enumerate(before(some)):
+            pz_ref[i + 1] = x
+        for i, x in enumerate(after):
+            oafter_ref[i] = x
+        wait_maps(1)
+        states = [got_ref[i, 1] for i in range(ROWS)]
+        ysend_ref[1] = total_added([oafter_ref[i] for i in range(7)], states)
+        @pl.when(y <= 2)
+        def _():
+            send_y(1, 1, 1).start()
+
+        @pl.when(y <= 1)
+        def _():
+            send_y(1, 2, 2).start()
+
+        pa_ref[0] = jnp.zeros((B, B), F32)
+        for i, x in enumerate(added(states, lambda name: oprod_ref[NAMES[name]])):
+            pa_ref[i + 1] = x
+        @pl.when(y >= 1)
+        def _():
+            send_y(1, 1, 1).wait_recv()
+
+        @pl.when(y >= 2)
+        def _():
+            send_y(0, 0, 1).wait_recv()
+            send_y(1, 2, 2).wait_recv()
+
+        s_row = ybuf_ref[1] + dotw(wide(ybuf_ref[0]), wide(ybuf_ref[2]))
         sh, sl = split(s_row)
         shh = jnp.concatenate([sh, sh], 0)
         for i in (4, 3, 5, 2, 6, 1, 7, 0):
             to = lax.rem(z + i, ROWS)
-            pm = pm_ref[to]
+            pm = pz_ref[to]
             sout_ref[to] = pa_ref[to] + dotf(pm, shh) + dotf(pm[:, :B], sl)
             if i:
                 send_state(i).start()
@@ -390,6 +485,18 @@
     def _():
         for i in range(1, ROWS):
             send_state(i).wait_send()
+
+        @pl.when((y == 1) | (y == 2))
+        def _():
+            send_y(0, 0, 1).wait_send()
+
+        @pl.when(y <= 2)
+        def _():
+            send_y(1, 1, 1).wait_send()
+
+        @pl.when(y <= 1)
+        def _():
+            send_y(1, 2, 2).wait_send()
 
 
 def local(queries, key_vectors, value_vectors, write_rates, doc_lengths, norm_gain):
@@ -409,14 +516,17 @@
             pltpu.VMEM((B, B), F32),
             pltpu.VMEM((B, B), F32),
             pltpu.VMEM((2, NB, B, 2 * B), F32),
-            pltpu.VMEM((2, NB, B, 2 * B), F32),
-            pltpu.VMEM((2, 5, B, 2 * B), F32),
+            pltpu.VMEM((2, 7, B, 2 * B), BF16),
+            pltpu.VMEM((2, 8, B, 2 * B), BF16),
+            pltpu.VMEM((2, NB, B, B), F32),
             pltpu.VMEM((2, 2, B, B), F32),
             pltpu.VMEM((ROWS, 2, B, B), F32),
             pltpu.VMEM((3, B, B), F32),
             pltpu.VMEM((2, B, B), F32),
             pltpu.VMEM((ROWS, B, 2 * B), BF16),
             pltpu.VMEM((ROWS, B, B), F32),
+            pltpu.VMEM((8, B, 2 * B), BF16),
+            pltpu.VMEM((7, B, 2 * B), BF16),
             pltpu.VMEM((ROWS, B, B), F32),
             pltpu.VMEM((2, B, B), F32),
             pltpu.VMEM((2, NB * B, 2 * B), BF16),

time: 42.8 us -> 39.2 us (0.916)
  the two profiles are of different devices: /device:TPU:1 before, /device:TPU:57 now
where the time goes in v4:
time: 39.2 us; the launch traced here: 39 us
  Pallas kernels  38.2 us (97%)
  local copies, waits for them, and re-layouts  0.8 us (2%)
    pallas_call x1, Pallas kernels, local(): pl.pallas_call(kernel, out_shape=pltpu.VMEM(queries.shape, BF16), in_spec...  38.2 us
    unnamed x1, local copies, waits for them, and re-layouts  0.8 us

profile of v4, /device:TPU:57, one launch (start us, length us, event | category | flops | bytes accessed | tf_op | source)
XLA Modules:
  0.0 39.0 jit_solution(8338158471051464862)
XLA Ops:
  0.0 38.2 %shard_map.64 = bf16[1024,256]{1,0:T(8,128)(2,1)S(1)} custom-call(s32[32]{0:T(128)} %doc_ref.1, bf16[1024,256]{1,0:T(8,128)(2,1)} %q_hbm.1, bf16[1024,256]{1,0:T(8,128)(2,1)} %k_hbm.1, bf16[1024,256]{1,0:T(8,128)(2,1)} %v_hbm.1, f32[2,1024]{1,0:T(2,128)} %bitcast.2, f32[1,256]{1,0:T(1,128)} %bitcast.3), custom_call_target="tpu_custom_call" | custom-call | tf_op jit(solution)/shard_map/pallas_call | solution.py:504
  38.3 0.8 %copy.8 = bf16[1024,256]{1,0:T(8,128)(2,1)} copy(bf16[1024,256]{1,0:T(8,128)(2,1)S(1)} %shard_map.64) | data formatting | bytes 1048576

commit v5 on v4

--- a/solution.py
+++ b/solution.py
@@ -158,7 +158,7 @@
 
 def kernel(
     doc_ref, q_hbm, k_hbm, v_hbm, rate_hbm, gain_hbm, o_ref,
-    q_ref, k_ref, v_ref, rate_ref, gain_ref, cols_ref, scale_ref, wu_ref, bm_ref, prod_ref, add_ref, mat_ref, got_ref, ybuf_ref, ysend_ref, pz_ref, pa_ref, oprod_ref, oafter_ref,
+    q_ref, k_ref, v_ref, rate_ref, gain_ref, cols_ref, end_ref, scale_ref, wu_ref, prod_ref, add_ref, mat_ref, got_ref, ybuf_ref, ysend_ref, pz_ref, pa_ref, oprod_ref, oafter_ref,
     sout_ref, sbuf_ref, qp_ref, o1_ref, xsend_ref, xbuf_ref,
     in_sem, g_send, g_recv, y_send, y_recv, s_send, s_recv, x_send, x_recv,
 ):
@@ -176,8 +176,8 @@
         load(5, gain_hbm, gain_ref, None),
         load(6, q_hbm, q_ref, None),
     ]
-    for copy in loads:
-        copy.start()
+    for i in (1, 0, 3, 2, 4, 5, 6):
+        loads[i].start()
     ctx, head = lax.axis_index("ctx"), lax.axis_index("head")
     y, z = ctx // ROWS, lax.rem(ctx, ROWS)
     core = lax.rem(head, 2)
@@ -206,9 +206,13 @@
     pos = base + iota((NB, B), 0) * B + iota((NB, B), 1)
     begin = jnp.int32(0)
     start = jnp.zeros((NB, B), jnp.int32)
+    end = jnp.full((NB, B), doc_ref[0])
     for m in range(31):
         begin = begin + doc_ref[m]
-        start = jnp.where(pos >= begin, begin, start)
+        passed = pos >= begin
+        start = jnp.where(passed, begin, start)
+        end = jnp.where(passed, begin + doc_ref[m + 1], end)
+    end_ref[...] = (end - base - iota((NB, B), 0) * B).astype(F32)
     loads[0].wait()
     rates = [rate_ref[h : h + 1, b * B : b * B + B] for h in range(2) for b in range(NB)]
     start_f = (start - base).astype(F32)
@@ -216,14 +220,23 @@
 
     row, col = iota((B, B), 0), iota((B, B), 1)
     eye = (row == col).astype(F32)
-    row1 = iota((B, 1), 0).astype(F32)
-    colf = col.astype(F32)
-
-    def doc_columns(b):
-        first = cols_ref[:, b : b + 1]
-        carry = (first < float(b * B)).astype(F32)
-        last = (row1 + float(b * B) >= first[B - 1 : B]).astype(F32)
-        return first, carry, last
+    rowf = row.astype(F32)
+    ones2 = jnp.ones((2 * B, B), BF16)
+
+    def same_doc(b):
+        return rowf < end_ref[b : b + 1]
+
+    def carried(b):
+        return (cols_ref[:, b : b + 1] < float(b * B)).astype(F32)
+
+    def unbroken(b):
+        return (cols_ref[B - 1 : B, b : b + 1] < float(b * B)).astype(F32)
+
+    def last_keys(b, kt):
+        return jnp.where(end_ref[b : b + 1] >= float(B), kt.astype(F32), 0.0).astype(BF16)
+
+    def norms(x):
+        return lax.rsqrt(dotf(wide(x * x), ones2) + EPS)
 
     def lanes(h):
         return pl.ds(pl.multiple_of(h * B, B), B)
@@ -237,9 +250,8 @@
         for b in range(NB):
             kb = k_ref[pl.ds(b * B, B), lanes(h)]
             kf = kb.astype(F32)
-            rk = lax.rsqrt(jnp.sum(kf * kf, axis=1, keepdims=True) + EPS)
-            first, _, _ = doc_columns(b)
-            keep = (row > col) & (colf + float(b * B) >= first)
+            rk = norms(kf)
+            keep = (row > col) & same_doc(b)
             scale = rate(b, h) * rk
             scales.append(scale)
             lows.append(jnp.where(keep, dot_nt(kb, kb) * (scale * rk), 0.0))
@@ -248,14 +260,11 @@
         ws = [dotw(inv[b], rights[b]) for b in range(NB)]
         ms, kts = [], []
         for b in range(NB):
-            _, carry, last = doc_columns(b)
-            w = ws[b] * carry
-            wu_ref[h, b, :, :B] = w
-            hi, lo = split(w * last)
+            wu_ref[h, b, :, :B] = ws[b]
             kt = k_ref[pl.ds(b * B, B), lanes(h)].T
-            kts.append(jnp.concatenate([kt, kt], 1))
-            m = dotf(kts[b], jnp.concatenate([hi, lo], 0))
-            ms.append(jnp.where(row == col, carry[B - 1 : B], 0.0) - m)
+            m = dotf(jnp.concatenate([kt, kt], 1), jnp.concatenate(split(ws[b]), 0))
+            ms.append((eye - m) * unbroken(b))
+            kts.append(kt)
         total, after, some = products(ms)
         mat_ref[h, 0] = total
         return inv, scales, kts, after, some
@@ -267,10 +276,9 @@
             us.append(dotw(inv[b], wide(vf * scales[b])))
         adds = []
         for b in range(NB):
-            _, _, last = doc_columns(b)
             wu_ref[h, b, :, B:] = us[b]
-            hi, lo = split(us[b] * last)
-            adds.append(dotf(kts[b], jnp.concatenate([hi, lo], 0)))
+            kt = last_keys(b, kts[b])
+            adds.append(dotf(jnp.concatenate([kt, kt], 1), jnp.concatenate(split(us[b]), 0)))
             add_ref[h, b] = adds[b]
         mat_ref[h, 1] = total_added(after, adds)
 
@@ -299,40 +307,39 @@
     def _():
         ybuf_ref[1] = jnp.zeros((B, B), F32)
 
-    left = []
-    for h in range(2):
-        loads[1 + 2 * h].wait()
-        left.append(own_product(h))
-        if h == 0:
-            pl.semaphore_wait(barrier, 17)
-        give(h, 0)
-    for h in range(2):
-        loads[2 + 2 * h].wait()
-        own_added(h, *left[h][:4])
-        give(h, 1)
-    for h in range(2):
+    loads[1].wait()
+    left = [own_product(0)]
+    pl.semaphore_wait(barrier, 17)
+    give(0, 0)
+    loads[3].wait()
+    left.append(own_product(1))
+    give(1, 0)
+    loads[2].wait()
+    loads[4].wait()
+    own_added(0, *left[0][:4])
+    own_added(1, *left[1][:4])
+    give(0, 1)
+    give(1, 1)
+
+    def shadow(h):
         keep_products(prod_ref.at[h], left[h][4])
-        for i, x in enumerate(before(left[h][4])):
-            bm_ref[h, i] = x
-
-    def shadow(h):
+        bms = before(left[h][4])
         adds = added([add_ref[h, b] for b in range(NB)], lambda name: prod_ref[h, NAMES[name]])
         scores, lefts = [], []
         for b in range(NB):
             kb = k_ref[pl.ds(b * B, B), lanes(h)]
             qb = q_ref[pl.ds(b * B, B), lanes(h)]
             qf = qb.astype(F32)
-            rq = lax.rsqrt(jnp.sum(qf * qf, axis=1, keepdims=True) + EPS)
-            first, carry, _ = doc_columns(b)
-            keep = (row >= col) & (colf + float(b * B) >= first)
+            rq = norms(qf)
+            keep = (row >= col) & same_doc(b)
             scores.append(jnp.where(keep, dot_nt(qb, kb) * rq, 0.0))
-            lefts.append(qf * (rq * carry))
+            lefts.append(qf * rq)
         both = [dot3(split(scores[b]), split(wu_ref[h, b])) for b in range(NB)]
-        qes = [lefts[b] - both[b][:, :B] for b in range(NB)]
+        qes = [(lefts[b] - both[b][:, :B]) * carried(b) for b in range(NB)]
         o1s = [both[b][:, B:] for b in range(NB)]
         qxs = []
         for b in range(1, NB):
-            bm, (ah, al) = bm_ref[h, b - 1], split(adds[b - 1])
+            bm, (ah, al) = bms[b - 1], split(adds[b - 1])
             right = (
                 jnp.concatenate([bm[:, :B], ah], 1),
                 jnp.concatenate([bm[:, B:], al], 1),
@@ -348,9 +355,7 @@
 
     loads[5].wait()
     loads[6].wait()
-    for h in range(2):
-        shadow(h)
-
+    shadow(0)
     def send_y(src, slot, step):
         return pltpu.make_async_remote_copy(
             src_ref=ysend_ref.at[src], dst_ref=ybuf_ref.at[slot],
@@ -401,6 +406,11 @@
         def _():
             send_y(1, 2, 2).start()
 
+    shadow(1)
+
+    @pl.when(mine)
+    def _():
+        states = [got_ref[i, 1] for i in range(ROWS)]
         pa_ref[0] = jnp.zeros((B, B), F32)
         for i, x in enumerate(added(states, lambda name: oprod_ref[NAMES[name]])):
             pa_ref[i + 1] = x
@@ -514,9 +524,9 @@
             pltpu.VMEM((2, NB * B), F32),
             pltpu.VMEM((1, 2 * B), F32),
             pltpu.VMEM((B, B), F32),
+            pltpu.VMEM((NB, B), F32),
             pltpu.VMEM((B, B), F32),
             pltpu.VMEM((2, NB, B, 2 * B), F32),
-            pltpu.VMEM((2, 7, B, 2 * B), BF16),
             pltpu.VMEM((2, 8, B, 2 * B), BF16),
             pltpu.VMEM((2, NB, B, B), F32),
             pltpu.VMEM((2, 2, B, B), F32),

time: 39.2 us -> 37.9 us (0.967)
  the two profiles are of different devices: /device:TPU:57 before, /device:TPU:1 now
where the time goes in v5:
time: 37.9 us; the launch traced here: 37.4 us
  Pallas kernels  36.6 us (97%)
  local copies, waits for them, and re-layouts  0.8 us (2%)
    pallas_call x1, Pallas kernels, local(): pl.pallas_call(kernel, out_shape=pltpu.VMEM(queries.shape, BF16), in_spec...  36.6 us
    unnamed x1, local copies, waits for them, and re-layouts  0.8 us

profile of v5, /device:TPU:1, one launch (start us, length us, event | category | flops | bytes accessed | tf_op | source)
XLA Modules:
  0.0 37.4 jit_solution(6781082069344924625)
XLA Ops:
  0.0 36.6 %shard_map.64 = bf16[1024,256]{1,0:T(8,128)(2,1)S(1)} custom-call(s32[32]{0:T(128)} %doc_ref.1, bf16[1024,256]{1,0:T(8,128)(2,1)} %q_hbm.1, bf16[1024,256]{1,0:T(8,128)(2,1)} %k_hbm.1, bf16[1024,256]{1,0:T(8,128)(2,1)} %v_hbm.1, f32[2,1024]{1,0:T(2,128)} %bitcast.2, f32[1,256]{1,0:T(1,128)} %bitcast.3), custom_call_target="tpu_custom_call" | custom-call | tf_op jit(solution)/shard_map/pallas_call | solution.py:514
  36.6 0.8 %copy.8 = bf16[1024,256]{1,0:T(8,128)(2,1)} copy(bf16[1024,256]{1,0:T(8,128)(2,1)S(1)} %shard_map.64) | data formatting | bytes 1048576

commit v6 on v5

--- a/solution.py
+++ b/solution.py
@@ -363,8 +363,7 @@
             device_id=at_y(y + step), device_id_type=MESH,
         )
 
-    def send_state(i):
-        to = lax.rem(z + i, ROWS)
+    def send_state(to):
         return pltpu.make_async_remote_copy(
             src_ref=sout_ref.at[to], dst_ref=sbuf_ref.at[my_h],
             send_sem=s_send.at[to], recv_sem=s_recv.at[my_h],
@@ -426,12 +425,14 @@
         s_row = ybuf_ref[1] + dotw(wide(ybuf_ref[0]), wide(ybuf_ref[2]))
         sh, sl = split(s_row)
         shh = jnp.concatenate([sh, sh], 0)
-        for i in (4, 3, 5, 2, 6, 1, 7, 0):
-            to = lax.rem(z + i, ROWS)
+        for to in (1, 2, 0, 3, 4, 7, 6, 5):
             pm = pz_ref[to]
             sout_ref[to] = pa_ref[to] + dotf(pm, shh) + dotf(pm[:, :B], sl)
-            if i:
-                send_state(i).start()
+
+            @pl.when(z != to)
+            def _():
+                send_state(to).start()
+
         sbuf_ref[my_h] = sout_ref[z]
 
     for h in range(2):
@@ -494,7 +495,7 @@
     @pl.when(mine)
     def _():
         for i in range(1, ROWS):
-            send_state(i).wait_send()
+            send_state(lax.rem(z + i, ROWS)).wait_send()
 
         @pl.when((y == 1) | (y == 2))
         def _():

time: 37.9 us -> 37.2 us (0.982); the launches traced: 37.4 us -> 37.1 us
  no operation moved by 1% of the time
where the time goes in v6:
time: 37.2 us; the launch traced here: 37.1 us
  Pallas kernels  36.3 us (98%)
  local copies, waits for them, and re-layouts  0.8 us (2%)
    pallas_call x1, Pallas kernels, local(): pl.pallas_call(kernel, out_shape=pltpu.VMEM(queries.shape, BF16), in_spec...  36.3 us
    unnamed x1, local copies, waits for them, and re-layouts  0.8 us

profile of v6, /device:TPU:1, one launch (start us, length us, event | category | flops | bytes accessed | tf_op | source)
XLA Modules:
  0.0 37.1 jit_solution(7412087976220259051)
XLA Ops:
  0.0 36.3 %shard_map.64 = bf16[1024,256]{1,0:T(8,128)(2,1)S(1)} custom-call(s32[32]{0:T(128)} %doc_ref.1, bf16[1024,256]{1,0:T(8,128)(2,1)} %q_hbm.1, bf16[1024,256]{1,0:T(8,128)(2,1)} %k_hbm.1, bf16[1024,256]{1,0:T(8,128)(2,1)} %v_hbm.1, f32[2,1024]{1,0:T(2,128)} %bitcast.2, f32[1,256]{1,0:T(1,128)} %bitcast.3), custom_call_target="tpu_custom_call" | custom-call | tf_op jit(solution)/shard_map/pallas_call | solution.py:515
  36.3 0.8 %copy.8 = bf16[1024,256]{1,0:T(8,128)(2,1)} copy(bf16[1024,256]{1,0:T(8,128)(2,1)S(1)} %shard_map.64) | data formatting | bytes 1048576
